TPU v7x, 32 devices: a whole 2x2x4 slice. The times are simulated.
32 devices in a mesh: dp: 8 (over z, x), tensor: 4 (over y, core).
Axes of the slice: x: 2, y: 2, z: 4, core: 2. Of those that a mesh axis runs over, the one named last changes fastest.
Arguments:
- tokens: bfloat16 [2, 8192, 1024], P(None, ('dp', 'tensor')), may hold values from -6 to 6
- condition: bfloat16 [2, 8, 1024], P(None, 'dp'), may hold values from -6 to 6
- cotangent: bfloat16 [2, 8192, 1024], P(None, ('dp', 'tensor')), may hold values from -6 to 6
- adaptive_weight: bfloat16 [6, 1024, 1024], P(None, 'dp', 'tensor'), may hold values from -0.1875 to 0.1875
- adaptive_bias: bfloat16 [6, 1024], P(None, ('tensor', 'dp')), may hold values from -1.796875 to 1.796875
- inward_weight: bfloat16 [1024, 16, 192], P('dp', 'tensor'), may hold values from -0.1875 to 0.1875
- inward_bias: bfloat16 [16, 128], P('tensor', 'dp'), may hold values from -1.796875 to 1.796875
- outward_weight: bfloat16 [16, 64, 1024], P('tensor', None, 'dp'), may hold values from -0.8984375 to 0.8984375
- outward_bias: bfloat16 [1024], P(('tensor', 'dp')), may hold values from -1.796875 to 1.796875
- expand_weight: bfloat16 [1024, 4096], P('dp', 'tensor'), may hold values from -0.1875 to 0.1875
- expand_bias: bfloat16 [4096], P(('tensor', 'dp')), may hold values from -1.796875 to 1.796875
- shrink_weight: bfloat16 [4096, 1024], P('tensor', 'dp'), may hold values from -0.09375 to 0.09375
- shrink_bias: bfloat16 [1024], P(('tensor', 'dp')), may hold values from -1.796875 to 1.796875
Outputs:
- result: bfloat16 [2, 8192, 1024], P(None, ('dp', 'tensor'))
- tokens_grad: float32 [2, 8192, 1024], P(None, ('dp', 'tensor'))
- condition_grad: float32 [2, 8, 1024], P(None, 'dp')
- adaptive_weight_grad: float32 [6, 1024, 1024], P(None, 'dp', 'tensor')
- adaptive_bias_grad: float32 [6, 1024], P(None, ('tensor', 'dp'))
- inward_weight_grad: float32 [1024, 16, 192], P('dp', 'tensor')
- inward_bias_grad: float32 [16, 128], P('tensor', 'dp')
- outward_weight_grad: float32 [16, 64, 1024], P('tensor', None, 'dp')
- outward_bias_grad: float32 [1024], P(('tensor', 'dp'))
- expand_weight_grad: float32 [1024, 4096], P('dp', 'tensor')
- expand_bias_grad: float32 [4096], P(('tensor', 'dp'))
- shrink_weight_grad: float32 [4096, 1024], P('tensor', 'dp')
- shrink_bias_grad: float32 [1024], P(('tensor', 'dp'))
All inputs are finite; a program needn't handle non-finite values.
Results may differ from a plain program's by a relative error of at most 0.02.
Values may be sent and summed in bfloat16 or wider, within the bound.
A program may use at most 256 MiB of HBM per device.

v0:
```python
import jax
import jax.numpy as jnp
from jax import lax
from jax.sharding import PartitionSpec as P

epsilon = 1e-06


def as_sent(array):

    def short(part):
        return part.astype(jnp.bfloat16) if part.dtype == jnp.float32 else part

    return jax.tree.map(short, array)


def normalize(value):
    centered = value - jnp.mean(value, axis=-1, keepdims=True)
    inverse = lax.rsqrt(jnp.mean(centered * centered, axis=-1, keepdims=True) + epsilon)
    return (centered * inverse, inverse)


def normalize_back(normed, inverse, grad_normed):
    first = jnp.mean(grad_normed, axis=-1, keepdims=True)
    second = jnp.mean(grad_normed * normed, axis=-1, keepdims=True)
    return inverse * (grad_normed - first - normed * second)


def gather_rows(value):
    return jax.tree.map(
        lambda part, own: part.astype(own.dtype),
        lax.all_gather(as_sent(value), "tensor", axis=0, tiled=True),
        value,
    )


def sum_rows(value):
    return lax.psum_scatter(
        value.astype(jnp.bfloat16), "tensor", scatter_dimension=0, tiled=True
    ).astype(jnp.float32)


def attend_forward(query, keys, values, block, scale):
    outputs = []
    totals = []
    for begin in range(0, query.shape[0], block):
        rows = query[begin : begin + block]
        scores = jnp.einsum("qhd,khd->hqk", rows, keys, preferred_element_type=jnp.float32) * scale
        peak = jnp.max(scores, axis=-1, keepdims=True)
        raised = jnp.exp(scores - peak)
        total = jnp.sum(raised, axis=-1, keepdims=True)
        weights = (raised / total).astype(jnp.bfloat16)
        outputs.append(
            jnp.einsum("hqk,khd->qhd", weights, values, preferred_element_type=jnp.float32)
        )
        totals.append(peak + jnp.log(total))
    return (jnp.concatenate(outputs, axis=0), jnp.concatenate(totals, axis=1))


def attend_backward(query, keys, values, logsum, grad_out, block, scale):
    grad_keys = jnp.zeros(keys.shape, jnp.float32)
    grad_values = jnp.zeros(values.shape, jnp.float32)
    grad_parts = []
    for begin in range(0, query.shape[0], block):
        rows = query[begin : begin + block]
        grad_rows = grad_out[begin : begin + block]
        scores = jnp.einsum("qhd,khd->hqk", rows, keys, preferred_element_type=jnp.float32) * scale
        weights = jnp.exp(scores - logsum[:, begin : begin + block])
        grad_weights = jnp.einsum(
            "qhd,khd->hqk", grad_rows, values, preferred_element_type=jnp.float32
        )
        inner = jnp.sum(grad_weights * weights, axis=-1, keepdims=True)
        grad_scores = (weights * (grad_weights - inner)).astype(jnp.bfloat16)
        grad_parts.append(
            jnp.einsum("hqk,khd->qhd", grad_scores, keys, preferred_element_type=jnp.float32)
            * scale
        )
        grad_keys = (
            grad_keys
            + jnp.einsum("hqk,qhd->khd", grad_scores, rows, preferred_element_type=jnp.float32)
            * scale
        )
        grad_values = grad_values + jnp.einsum(
            "hqk,qhd->khd",
            weights.astype(jnp.bfloat16),
            grad_rows,
            preferred_element_type=jnp.float32,
        )
    return (jnp.concatenate(grad_parts, axis=0), grad_keys, grad_values)


def body(
    tokens,
    condition,
    cotangent,
    adaptive_weight,
    adaptive_bias,
    inward_weight,
    inward_bias,
    outward_weight,
    outward_bias,
    expand_weight,
    expand_bias,
    shrink_weight,
    shrink_bias,
):
    tensor_size = lax.axis_size("tensor")
    micro, tok_rows, width = tokens.shape
    latents = condition.shape[1]
    group_rows = tok_rows * tensor_size
    seq_len = group_rows // latents
    heads_local = outward_weight.shape[0]
    head_size = outward_weight.shape[1]
    hidden_local = shrink_weight.shape[0]
    block = min(512, seq_len)
    scale = head_size ** (-0.5)

    def attn_params():
        return (
            lax.all_gather(inward_weight, "dp", axis=0, tiled=True),
            lax.all_gather(inward_bias, "dp", axis=1, tiled=True),
            lax.all_gather(outward_weight, "dp", axis=2, tiled=True),
        )

    def mlp_params():
        pieces = (
            lax.all_gather(expand_weight, "dp", axis=0, tiled=True),
            lax.all_gather(expand_bias, "dp", axis=0, tiled=True),
            lax.all_gather(shrink_weight, "dp", axis=1, tiled=True),
        )
        return pieces

    ada_full, ada_bias, outward_piece, shrink_piece = (
        lax.all_gather(adaptive_weight, "dp", axis=1, tiled=True),
        lax.all_gather(adaptive_bias, "dp", axis=1, tiled=True),
        lax.all_gather(outward_bias, "dp", axis=0, tiled=True),
        lax.all_gather(shrink_bias, "dp", axis=0, tiled=True),
    )
    cond_float = condition.astype(jnp.float32)
    cond_act = jax.nn.silu(cond_float).astype(jnp.bfloat16)
    mod_part = jnp.einsum(
        "bli,kio->blko", cond_act, ada_full, preferred_element_type=jnp.float32
    ) + ada_bias.astype(jnp.float32)
    modulation, proj_bias, out_bias = (
        lax.all_gather(mod_part, "tensor", axis=3, tiled=True),
        lax.all_gather(outward_piece.astype(jnp.float32), "tensor", axis=0, tiled=True),
        lax.all_gather(shrink_piece.astype(jnp.float32), "tensor", axis=0, tiled=True),
    )
    first_row = lax.axis_index("tensor") * tok_rows
    owner = (first_row + jnp.arange(tok_rows, dtype=jnp.int32)) // seq_len
    member = (owner[:, None] == jnp.arange(latents, dtype=jnp.int32)[None, :]).astype(jnp.float32)
    states = []
    outputs = []
    for index in range(micro):
        rows_mod = jnp.dot(
            member, modulation[index].reshape(latents, 6 * width), precision=lax.Precision.HIGHEST
        ).reshape(tok_rows, 6, width)
        inputs = tokens[index].astype(jnp.float32)
        normed_one, inverse_one = normalize(inputs)
        mixed_in = (normed_one * (1.0 + rows_mod[:, 1]) + rows_mod[:, 0]).astype(jnp.bfloat16)
        attn_weight, qv_bias, proj_weight = attn_params()
        mixed_full = gather_rows(mixed_in)
        qkv_bias = jnp.concatenate(
            [
                qv_bias[:, :head_size],
                jnp.zeros((heads_local, head_size), jnp.bfloat16),
                qv_bias[:, head_size:],
            ],
            axis=1,
        ).astype(jnp.float32)
        projected = jnp.dot(
            mixed_full,
            attn_weight.reshape(width, heads_local * 3 * head_size),
            preferred_element_type=jnp.float32,
        )
        packed = (projected.reshape(group_rows, heads_local, 3 * head_size) + qkv_bias).astype(
            jnp.bfloat16
        )
        packed_seq = packed.reshape(latents, seq_len, heads_local, 3 * head_size)
        query = packed_seq[..., :head_size]
        keys = packed_seq[..., head_size : 2 * head_size]
        values = packed_seq[..., 2 * head_size :]
        attended, logsum = lax.map(
            lambda item: attend_forward(item[0], item[1], item[2], block, scale),
            (query, keys, values),
        )
        attended = attended.astype(jnp.bfloat16).reshape(group_rows, heads_local * head_size)
        attn_terms = jnp.dot(
            attended,
            proj_weight.reshape(heads_local * head_size, width),
            preferred_element_type=jnp.float32,
        )
        attn_out = sum_rows(attn_terms) + proj_bias
        first_sum = inputs + rows_mod[:, 2] * attn_out
        normed_two, inverse_two = normalize(first_sum)
        mlp_in = (normed_two * (1.0 + rows_mod[:, 4]) + rows_mod[:, 3]).astype(jnp.bfloat16)
        fc_in, fc_bias, fc_out = mlp_params()
        state = {}
        mlp_full = gather_rows(mlp_in)
        hidden = jnp.dot(mlp_full, fc_in, preferred_element_type=jnp.float32) + fc_bias.astype(
            jnp.float32
        )
        active = jax.nn.gelu(hidden, approximate=True).astype(jnp.bfloat16)
        mlp_out = sum_rows(jnp.dot(active, fc_out, preferred_element_type=jnp.float32)) + out_bias
        outputs.append((first_sum + rows_mod[:, 5] * mlp_out).astype(jnp.bfloat16))
        state.update(
            {
                "rows_mod": rows_mod,
                "normed_one": normed_one,
                "inverse_one": inverse_one,
                "mixed_in": mixed_in,
                "query": query,
                "keys": keys,
                "values": values,
                "logsum": logsum,
                "attended": attended,
                "attn_out": attn_out,
                "normed_two": normed_two,
                "inverse_two": inverse_two,
                "mlp_in": mlp_in,
                "hidden": hidden,
                "active": active,
                "mlp_out": mlp_out,
            }
        )
        states.append(state)
    acc_qkv = jnp.zeros((width, heads_local, 3 * head_size), jnp.float32)
    acc_qv = jnp.zeros((heads_local, 2 * head_size), jnp.float32)
    acc_proj = jnp.zeros((heads_local, head_size, width), jnp.float32)
    acc_proj_bias = jnp.zeros((width,), jnp.float32)
    acc_fc_in = jnp.zeros((width, hidden_local), jnp.float32)
    acc_fc_bias = jnp.zeros((hidden_local,), jnp.float32)
    acc_fc_out = jnp.zeros((hidden_local, width), jnp.float32)
    acc_out_bias = jnp.zeros((width,), jnp.float32)
    mod_grads = []
    token_grads = []
    for index in range(micro):
        state = states[index]
        rows_mod = state["rows_mod"]
        attn_weight, qv_bias, proj_weight = attn_params()
        fc_in, fc_bias, fc_out = mlp_params()
        mixed_full = gather_rows(state["mixed_in"])
        grad_two = cotangent[index].astype(jnp.float32)
        grad_mlp = (rows_mod[:, 5] * grad_two).astype(jnp.bfloat16)
        acc_out_bias = acc_out_bias + jnp.sum(grad_mlp, axis=0, dtype=jnp.float32)
        unused, pull = jax.vjp(lambda value: jax.nn.gelu(value, approximate=True), state["hidden"])
        mlp_full = gather_rows(state["mlp_in"])
        grad_mlp_full = gather_rows(grad_mlp)
        acc_fc_out = acc_fc_out + jnp.einsum(
            "th,to->ho", state["active"], grad_mlp_full, preferred_element_type=jnp.float32
        )
        grad_active = jnp.einsum(
            "to,ho->th", grad_mlp_full, fc_out, preferred_element_type=jnp.float32
        )
        grad_hidden = pull(grad_active)[0].astype(jnp.bfloat16)
        acc_fc_bias = acc_fc_bias + jnp.sum(grad_hidden, axis=0, dtype=jnp.float32)
        acc_fc_in = acc_fc_in + jnp.einsum(
            "ti,th->ih", mlp_full, grad_hidden, preferred_element_type=jnp.float32
        )
        grad_mlp_in = sum_rows(
            jnp.einsum("th,ih->ti", grad_hidden, fc_in, preferred_element_type=jnp.float32)
        )
        normed_two = state["normed_two"]
        grad_first = grad_two + normalize_back(
            normed_two, state["inverse_two"], grad_mlp_in * (1.0 + rows_mod[:, 4])
        )
        grad_attn = (rows_mod[:, 2] * grad_first).astype(jnp.bfloat16)
        acc_proj_bias = acc_proj_bias + jnp.sum(grad_attn, axis=0, dtype=jnp.float32)
        grad_attn_full = gather_rows(grad_attn)
        acc_proj = acc_proj + jnp.einsum(
            "tc,to->co", state["attended"], grad_attn_full, preferred_element_type=jnp.float32
        ).reshape(heads_local, head_size, width)
        grad_attended = jnp.einsum(
            "to,co->tc",
            grad_attn_full,
            proj_weight.reshape(heads_local * head_size, width),
            preferred_element_type=jnp.float32,
        ).astype(jnp.bfloat16)
        grad_attended = grad_attended.reshape(latents, seq_len, heads_local, head_size)
        grad_query, grad_keys, grad_values = lax.map(
            lambda item: attend_backward(item[0], item[1], item[2], item[3], item[4], block, scale),
            (state["query"], state["keys"], state["values"], state["logsum"], grad_attended),
        )
        grad_packed = jnp.concatenate([grad_query, grad_keys, grad_values], axis=-1).astype(
            jnp.bfloat16
        )
        grad_packed = grad_packed.reshape(group_rows, heads_local, 3 * head_size)
        summed = jnp.sum(grad_packed, axis=0, dtype=jnp.float32)
        acc_qv = acc_qv + jnp.concatenate(
            [summed[:, :head_size], summed[:, 2 * head_size :]], axis=1
        )
        acc_qkv = acc_qkv + jnp.einsum(
            "ti,thc->ihc", mixed_full, grad_packed, preferred_element_type=jnp.float32
        )
        grad_mixed = sum_rows(
            jnp.einsum("thc,ihc->ti", grad_packed, attn_weight, preferred_element_type=jnp.float32)
        )
        normed_one = state["normed_one"]
        token_grads.append(
            grad_first
            + normalize_back(normed_one, state["inverse_one"], grad_mixed * (1.0 + rows_mod[:, 1]))
        )
        rows_grad = jnp.stack(
            [
                grad_mixed,
                grad_mixed * normed_one,
                grad_first * state["attn_out"],
                grad_mlp_in,
                grad_mlp_in * normed_two,
                grad_two * state["mlp_out"],
            ],
            axis=1,
        )
        mod_grads.append(
            jnp.einsum(
                "tl,tc->lc",
                member,
                rows_grad.reshape(tok_rows, 6 * width),
                precision=lax.Precision.HIGHEST,
            ).reshape(latents, 6, width)
        )
    mod_share, proj_bias_share, out_bias_share = (
        lax.psum_scatter(
            jnp.stack(mod_grads).astype(jnp.bfloat16), "tensor", scatter_dimension=3, tiled=True
        ).astype(jnp.float32),
        lax.psum_scatter(
            acc_proj_bias.astype(jnp.bfloat16), "tensor", scatter_dimension=0, tiled=True
        ).astype(jnp.float32),
        lax.psum_scatter(
            acc_out_bias.astype(jnp.bfloat16), "tensor", scatter_dimension=0, tiled=True
        ).astype(jnp.float32),
    )
    mod_low = mod_share.astype(jnp.bfloat16)
    grad_ada = jnp.einsum("bli,blko->kio", cond_act, mod_low, preferred_element_type=jnp.float32)
    grad_ada_bias = jnp.sum(mod_low, axis=(0, 1), dtype=jnp.float32)
    cond_back = jnp.einsum("blko,kio->bli", mod_low, ada_full, preferred_element_type=jnp.float32)
    cond_total = lax.psum(cond_back.astype(jnp.bfloat16), "tensor").astype(jnp.float32)
    unused, pull_cond = jax.vjp(jax.nn.silu, cond_float)
    grad_cond = pull_cond(cond_total)[0]
    shares = (
        lax.psum_scatter(
            grad_ada.astype(jnp.bfloat16), "dp", scatter_dimension=1, tiled=True
        ).astype(jnp.float32),
        lax.psum_scatter(
            grad_ada_bias.astype(jnp.bfloat16), "dp", scatter_dimension=1, tiled=True
        ).astype(jnp.float32),
        lax.psum_scatter(
            acc_qkv.astype(jnp.bfloat16), "dp", scatter_dimension=0, tiled=True
        ).astype(jnp.float32),
        lax.psum_scatter(acc_qv.astype(jnp.bfloat16), "dp", scatter_dimension=1, tiled=True).astype(
            jnp.float32
        ),
        lax.psum_scatter(
            acc_proj.astype(jnp.bfloat16), "dp", scatter_dimension=2, tiled=True
        ).astype(jnp.float32),
        lax.psum_scatter(
            proj_bias_share.astype(jnp.bfloat16), "dp", scatter_dimension=0, tiled=True
        ).astype(jnp.float32),
        lax.psum_scatter(
            acc_fc_in.astype(jnp.bfloat16), "dp", scatter_dimension=0, tiled=True
        ).astype(jnp.float32),
        lax.psum_scatter(
            acc_fc_bias.astype(jnp.bfloat16), "dp", scatter_dimension=0, tiled=True
        ).astype(jnp.float32),
        lax.psum_scatter(
            acc_fc_out.astype(jnp.bfloat16), "dp", scatter_dimension=1, tiled=True
        ).astype(jnp.float32),
        lax.psum_scatter(
            out_bias_share.astype(jnp.bfloat16), "dp", scatter_dimension=0, tiled=True
        ).astype(jnp.float32),
    )
    return (
        jnp.stack(outputs),
        jnp.stack(token_grads),
        grad_cond,
        shares[0],
        shares[1],
        shares[2],
        shares[3],
        shares[4],
        shares[5],
        shares[6],
        shares[7],
        shares[8],
        shares[9],
    )


def solution(mesh):
    in_specs = (
        P(None, ("dp", "tensor"), None),
        P(None, "dp", None),
        P(None, ("dp", "tensor"), None),
        P(None, "dp", "tensor"),
        P(None, ("tensor", "dp")),
        P("dp", "tensor", None),
        P("tensor", "dp"),
        P("tensor", None, "dp"),
        P(("tensor", "dp")),
        P("dp", "tensor"),
        P(("tensor", "dp")),
        P("tensor", "dp"),
        P(("tensor", "dp")),
    )
    out_specs = (
        P(None, ("dp", "tensor"), None),
        P(None, ("dp", "tensor"), None),
        P(None, "dp", None),
        P(None, "dp", "tensor"),
        P(None, ("tensor", "dp")),
        P("dp", "tensor", None),
        P("tensor", "dp"),
        P("tensor", None, "dp"),
        P(("tensor", "dp")),
        P("dp", "tensor"),
        P(("tensor", "dp")),
        P("tensor", "dp"),
        P(("tensor", "dp")),
    )
    return jax.shard_map(body, mesh=mesh, in_specs=in_specs, out_specs=out_specs, check_vma=False)
```

profile of v0, /device:TPU:0, one launch (start us, length us, event | category | flops | bytes accessed | tf_op | source)
XLA Modules:
  0.0 1361.5 jit_solution(12362159846870158425)
XLA Ops:
  8.7 28.2 %all-gather.1 = bf16[8,32,6]{1,2,0:T(8,128)(2,1)S(1)} all-gather(bf16[1,32,6]{1,2,0:T(8,128)(2,1)} %bitcast.604), channel_id=1, replica_groups=mesh['dp'=8,'tensor'=4] {'dp'}, dimensions={0}, use_global_device_ids=true | all-gather | bytes 3456 | tf_op jit(solution)/shard_map/all_gather | solution.py:135
  39.7 33.8 %all-gather.19.cloned.1.call-done = bf16[6,1024,256]{2,1,0:T(8,128)(2,1)} async-done(((bf16[6,128,256]{2,1,0:T(8,128)(2,1)}), bf16[6,1024,256]{2,1,0:T(8,128)(2,1)}) %all-gather.19.cloned.1.call-update) | async-done | bytes 3145744 | tf_op jit(solution)/shard_map/all_gather | solution.py:134
  76.0 5.2 all-gather
  88.8 18.3 %all-gather.2 = bf16[8,16,4]{1,2,0:T(4,128)(2,1)S(1)} all-gather(bf16[1,16,4]{1,2,0:T(4,128)(2,1)S(1)} %bitcast.605), channel_id=1, replica_groups=mesh['dp'=8,'tensor'=4] {'dp'}, dimensions={0}, use_global_device_ids=true | all-gather | bytes 1152 | tf_op jit(solution)/shard_map/all_gather | solution.py:121
  107.3 28.3 %all_gather.87 = bf16[4,64,1024]{2,1,0:T(8,128)(2,1)S(1)} all-gather(bf16[4,64,128]{2,1,0:T(8,128)(2,1)S(1)} %copy-done.33), channel_id=1, replica_groups=mesh['dp'=8,'tensor'=4] {'dp'}, dimensions={2}, use_global_device_ids=true | all-gather | bytes 589824 | tf_op jit(solution)/shard_map/all_gather | solution.py:122
  135.7 13.0 all-gather.31.cloned.1.call-done
  148.6 3.9 fusion.55
  168.2 21.4 %all-reduce = bf16[256]{0:T(256)(128)(2,1)S(1)} all-reduce(bf16[256]{0:T(256)(128)(2,1)S(1)} %dynamic-update-slice), channel_id=1, replica_groups=mesh['dp'=8,'tensor'=4] {'dp'}, use_global_device_ids=true, to_apply=%add | all-reduce | flops 256 | bytes 1024
  189.5 5.1 all-gather.3
  199.5 3.8 convert_reduce_fusion.6
  204.8 20.4 %all-gather.4 = bf16[8,1,128]{2,1,0:T(2,128)(2,1)S(1)} all-gather(bf16[1,1,128]{2,1,0:T(2,128)(2,1)S(1)} %bitcast.608), channel_id=1, replica_groups=mesh['dp'=8,'tensor'=4] {'dp'}, dimensions={0}, use_global_device_ids=true | all-gather | bytes 2304 | tf_op jit(solution)/shard_map/all_gather | solution.py:128
  225.2 23.8 %all-gather.27.cloned.1.call-done = bf16[1024,1024]{1,0:T(8,128)(2,1)} async-done(((bf16[128,1024]{1,0:T(8,128)(2,1)}), bf16[1024,1024]{1,0:T(8,128)(2,1)}) %all-gather.27.cloned.1.call-update) | async-done | bytes 2097168 | tf_op jit(solution)/shard_map/all_gather | solution.py:127
  249.0 23.2 %all-gather.33.cloned.1.call-done = bf16[1024,1024]{1,0:T(8,128)(2,1)} async-done(((bf16[256,1024]{1,0:T(8,128)(2,1)}), bf16[1024,1024]{1,0:T(8,128)(2,1)}) %all-gather.33.cloned.1.call-update) | async-done | bytes 2097168 | tf_op jit(solution)/shard_map/all_gather | solution.py:32
  272.2 6.6 fusion.225
  278.7 46.8 %all-gather.29.cloned.1.call-done = bf16[1024,1024]{1,0:T(8,128)(2,1)} async-done(((bf16[1024,128]{1,0:T(8,128)(2,1)}), bf16[1024,1024]{1,0:T(8,128)(2,1)}) %all-gather.29.cloned.1.call-update) | async-done | bytes 2097168 | tf_op jit(solution)/shard_map/all_gather | solution.py:129
  325.5 23.0 %all-gather.39.cloned.1.call-done = bf16[1024,1024]{1,0:T(8,128)(2,1)} async-done(((bf16[256,1024]{1,0:T(8,128)(2,1)}), bf16[1024,1024]{1,0:T(8,128)(2,1)}) %all-gather.39.cloned.1.call-update) | async-done | bytes 2097168 | tf_op jit(solution)/shard_map/all_gather | solution.py:32
  348.5 9.0 convert_reduce_fusion
  362.6 31.5 %reduce-scatter.41.cloned.1.call-done = bf16[256,1024]{1,0:T(8,128)(2,1)} async-done(((bf16[1024,1024]{1,0:T(8,128)(2,1)}), bf16[256,1024]{1,0:T(8,128)(2,1)}) %reduce-scatter.41.cloned.1.call-update) | async-done | bytes 524304 | tf_op jit(solution)/shard_map/reduce_scatter | solution.py:38
  395.9 3.9 convert_reduce_fusion.8
  400.2 22.5 %all-gather.41.cloned.1.call-done = bf16[1024,1024]{1,0:T(8,128)(2,1)} async-done(((bf16[256,1024]{1,0:T(8,128)(2,1)}), bf16[1024,1024]{1,0:T(8,128)(2,1)}) %all-gather.41.cloned.1.call-update) | async-done | bytes 2097168 | tf_op jit(solution)/shard_map/all_gather | solution.py:32
  425.1 7.7 multiply_reduce_fusion.1
  432.9 4.6 multiply_convert_fusion.1
  439.8 4.5 multiply_reduce_fusion
  446.2 4.5 multiply_convert_fusion
  460.6 31.1 %reduce-scatter.43.cloned.1.call-done = bf16[256,1024]{1,0:T(8,128)(2,1)} async-done(((bf16[1024,1024]{1,0:T(8,128)(2,1)}), bf16[256,1024]{1,0:T(8,128)(2,1)}) %reduce-scatter.43.cloned.1.call-update) | async-done | bytes 524304 | tf_op jit(solution)/shard_map/reduce_scatter | solution.py:38
  496.9 22.7 %all-gather.21.cloned.1.call-done = bf16[1024,1024]{1,0:T(8,128)(2,1)} async-done(((bf16[256,1024]{1,0:T(8,128)(2,1)}), bf16[1024,1024]{1,0:T(8,128)(2,1)}) %all-gather.21.cloned.1.call-update) | async-done | bytes 2097168 | tf_op jit(solution)/shard_map/all_gather | solution.py:32
  537.1 31.5 %reduce-scatter.29.cloned.1.call-done = bf16[256,1024]{1,0:T(8,128)(2,1)} async-done(((bf16[1024,1024]{1,0:T(8,128)(2,1)}), bf16[256,1024]{1,0:T(8,128)(2,1)}) %reduce-scatter.29.cloned.1.call-update) | async-done | bytes 524304 | tf_op jit(solution)/shard_map/reduce_scatter | solution.py:38
  574.5 21.9 %all-gather.25.cloned.1.call-done = bf16[1024,1024]{1,0:T(8,128)(2,1)} async-done(((bf16[256,1024]{1,0:T(8,128)(2,1)}), bf16[1024,1024]{1,0:T(8,128)(2,1)}) %all-gather.25.cloned.1.call-update) | async-done | bytes 2097168 | tf_op jit(solution)/shard_map/all_gather | solution.py:32
  596.4 6.5 fusion.224
  602.9 18.1 %all-gather.35.cloned.1.call-done = bf16[1024,1024]{1,0:T(8,128)(2,1)} async-done(((bf16[256,1024]{1,0:T(8,128)(2,1)}), bf16[1024,1024]{1,0:T(8,128)(2,1)}) %all-gather.35.cloned.1.call-update) | async-done | bytes 2097168 | tf_op jit(solution)/shard_map/all_gather | solution.py:32
  621.0 8.4 convert_reduce_fusion.1
  634.5 31.5 %reduce-scatter.37.cloned.1.call-done = bf16[256,1024]{1,0:T(8,128)(2,1)} async-done(((bf16[1024,1024]{1,0:T(8,128)(2,1)}), bf16[256,1024]{1,0:T(8,128)(2,1)}) %reduce-scatter.37.cloned.1.call-update) | async-done | bytes 524304 | tf_op jit(solution)/shard_map/reduce_scatter | solution.py:38
  671.5 22.4 %all-gather.37.cloned.1.call-done = bf16[1024,1024]{1,0:T(8,128)(2,1)} async-done(((bf16[256,1024]{1,0:T(8,128)(2,1)}), bf16[1024,1024]{1,0:T(8,128)(2,1)}) %all-gather.37.cloned.1.call-update) | async-done | bytes 2097168 | tf_op jit(solution)/shard_map/all_gather | solution.py:32
  696.5 7.7 multiply_reduce_fusion.3
  704.2 4.7 multiply_convert_fusion.3
  711.2 4.5 multiply_reduce_fusion.2
  717.6 4.5 multiply_convert_fusion.2
  731.5 7.1 convolution_convert_fusion.2
  738.7 7.4 convolution_convert_fusion.4
  748.8 7.9 fusion.208
  756.7 6.3 all-reduce.8
  763.2 21.6 %all-reduce.7 = (bf16[256]{0:T(256)(128)(2,1)S(1)}, bf16[256]{0:T(256)(128)(2,1)S(1)}, bf16[1024]{0:T(1024)(128)(2,1)S(1)}, bf16[256]{0:T(256)(128)(2,1)S(1)}) all-reduce(bf16[256]{0:T(256)(128)(2,1)S(1)} %dynamic-update-slice.1, bf16[256]{0:T(256)(128)(2,1)S(1)} %dynamic-slice.5, ...), channel_id=1, replica_groups=mesh['dp'=8,'tensor'=4] {'dp'}, use_global_device_ids=true, to_apply=%add.1 | all-reduce | flops 1792 | bytes 7168
  784.8 5.2 all-gather.5
  795.1 3.8 bitcast_dynamic-update-slice_fusion.1
  803.6 27.0 %reduce-scatter.31.cloned.1.call-done = bf16[256,1024]{1,0:T(8,128)(2,1)} async-done(((bf16[1024,1024]{1,0:T(8,128)(2,1)}), bf16[256,1024]{1,0:T(8,128)(2,1)}) %reduce-scatter.31.cloned.1.call-update) | async-done | bytes 524304 | tf_op jit(solution)/shard_map/reduce_scatter | solution.py:38
  833.9 6.6 copy.46
  840.5 5.7 fusion.6
  846.2 6.6 copy.47
  852.8 5.7 fusion.4
  859.2 8.5 add_convert_fusion
  867.7 3.9 copy.64
  871.9 4.8 fusion.226
  876.8 3.9 add_convert_fusion.1
  895.6 4.0 fusion.228
  911.0 6.6 copy.54
  917.7 4.9 copy.70
  924.0 26.3 %reduce-scatter.59.cloned.1.call-done = bf16[128,1024]{1,0:T(8,128)(2,1)} async-done(((bf16[1024,1024]{1,0:T(8,128)(2,1)}), bf16[128,1024]{1,0:T(8,128)(2,1)}) %reduce-scatter.59.cloned.1.call-update) | async-done | bytes 262160
  952.2 69.3 %reduce-scatter.47.cloned.1.call-done = bf16[128,1024]{1,0:T(8,128)(2,1)} async-done(((bf16[1024,1024]{1,0:T(8,128)(2,1)}), bf16[128,1024]{1,0:T(8,128)(2,1)}) %reduce-scatter.47.cloned.1.call-update) | async-done | bytes 262160 | tf_op jit(solution)/shard_map/reduce_scatter | solution.py:359
  1025.0 52.9 %reduce-scatter.55.cloned.1.call-done = bf16[16,4]{1,0:T(8,128)(2,1)} async-done(((bf16[128,4]{1,0:T(8,128)(2,1)}), bf16[16,4]{1,0:T(8,128)(2,1)}) %reduce-scatter.55.cloned.1.call-update) | async-done | bytes 144
  1079.2 63.8 %reduce-scatter.57.cloned.1.call-done = bf16[128,256]{1,0:T(8,128)(2,1)} async-done(((bf16[1024,256]{1,0:T(8,128)(2,1)}), bf16[128,256]{1,0:T(8,128)(2,1)}) %reduce-scatter.57.cloned.1.call-update) | async-done | bytes 65552
  1144.8 65.5 %reduce-scatter.53.cloned.1.call-done = bf16[128,768]{1,0:T(8,128)(2,1)} async-done(((bf16[1024,768]{1,0:T(8,128)(2,1)}), bf16[128,768]{1,0:T(8,128)(2,1)}) %reduce-scatter.53.cloned.1.call-update) | async-done | bytes 196624
  1221.7 5.7 psum.7
  1228.0 46.1 %reduce-scatter.51.cloned.1.call-done = bf16[32,6]{1,0:T(8,128)(2,1)} async-done(((bf16[256,6]{1,0:T(8,128)(2,1)}), bf16[32,6]{1,0:T(8,128)(2,1)}) %reduce-scatter.51.cloned.1.call-update) | async-done | bytes 400
  1275.5 75.9 %reduce-scatter.49.cloned.1.call-done = bf16[128,1536]{1,0:T(8,128)(2,1)} async-done(((bf16[1024,1536]{1,0:T(8,128)(2,1)}), bf16[128,1536]{1,0:T(8,128)(2,1)}) %reduce-scatter.49.cloned.1.call-update) | async-done | bytes 393232
  (354 shorter events, 181.4 us)
Async XLA Ops:
  7.2 66.4 %all-gather.19.cloned.1.call-start = ((), (), s32[]{:S(2)}) async-start(), calls=%async_computation.16 | async-start | bytes 3538944 | tf_op jit(solution)/shard_map/all_gather | solution.py:134
  7.9 127.7 %all-gather.23.cloned.1.call-start = ((), (), s32[]{:S(2)}) async-start(), calls=%async_computation.18 | async-start | bytes 1769472 | tf_op jit(solution)/shard_map/all_gather | solution.py:120
  8.7 140.0 %all-gather.31.cloned.1.call-start = ((), (), s32[]{:S(2)}) async-start(), calls=%async_computation.24 | async-start | bytes 2621440 | tf_op jit(solution)/shard_map/all_gather | solution.py:32
  81.2 6.3 copy-start.5
  81.3 7.5 copy-start.47
  81.3 26.0 %copy-start.33 = (bf16[4,64,128]{2,1,0:T(8,128)(2,1)S(1)}, bf16[4,64,128]{2,1,0:T(8,128)(2,1)}, u32[]{:S(2)}) copy-start(bf16[4,64,128]{2,1,0:T(8,128)(2,1)} %param.20) | copy-start | bytes 196612
  88.7 108.7 %reduce-scatter.33.cloned.1.call-start = ((), (), s32[]{:S(2)}) async-start(), calls=%async_computation.25 | async-start | bytes 2621440 | tf_op jit(solution)/shard_map/reduce_scatter | solution.py:38
  135.7 28.1 %copy-start.20 = (bf16[4,64,1024]{2,1,0:T(8,128)(2,1)}, bf16[4,64,1024]{2,1,0:T(8,128)(2,1)S(1)}, u32[]{:S(2)}) copy-start(bf16[4,64,1024]{2,1,0:T(8,128)(2,1)S(1)} %all_gather.87) | copy-start | bytes 1572868
  152.5 8.8 copy-start.8
  155.3 6.0 copy-start.1
  163.7 33.8 %copy-start.28 = (bf16[4,64,512]{2,1,0:T(8,128)(2,1)}, bf16[4,64,512]{2,1,0:T(8,128)(2,1)S(1)}, u32[]{:S(2)}) copy-start(bf16[4,64,512]{2,1,0:T(8,128)(2,1)S(1)} %fusion.114) | copy-start | bytes 786436
  163.8 35.7 %copy-start.13 = (bf16[2,256,1024]{2,1,0:T(8,128)(2,1)S(1)}, bf16[2,256,1024]{2,1,0:T(8,128)(2,1)}, u32[]{:S(2)}) copy-start(bf16[2,256,1024]{2,1,0:T(8,128)(2,1)} %param.15) | copy-start | bytes 3145732
  165.8 83.1 %all-gather.27.cloned.1.call-start = ((), (), s32[]{:S(2)}) async-start(), calls=%async_computation.21 | async-start | bytes 2359296 | tf_op jit(solution)/shard_map/all_gather | solution.py:127
  166.4 105.7 %all-gather.33.cloned.1.call-start = ((), (), s32[]{:S(2)}) async-start(), calls=%async_computation.26 | async-start | bytes 2621440 | tf_op jit(solution)/shard_map/all_gather | solution.py:32
  199.1 196.8 %copy-start.6 = (f32[256,1024]{1,0:T(8,128)}, f32[256,1024]{1,0:T(8,128)S(1)}, u32[]{:S(2)}) copy-start(f32[256,1024]{1,0:T(8,128)S(1)} %get-tuple-element.193) | copy-start | bytes 3145732
  199.2 196.7 %copy-start.36 = (f32[256]{0:T(256)}, f32[256]{0:T(256)S(1)}, u32[]{:S(2)}) copy-start(f32[256]{0:T(256)S(1)} %broadcast_multiply_fusion.10) | copy-start | bytes 3076
  199.4 196.5 %copy-start.38 = (f32[256]{0:T(256)}, f32[256]{0:T(256)S(1)}, u32[]{:S(2)}) copy-start(f32[256]{0:T(256)S(1)} %add_rsqrt_fusion) | copy-start | bytes 3076
  203.2 122.3 %all-gather.29.cloned.1.call-start = ((), (), s32[]{:S(2)}) async-start(), calls=%async_computation.22 | async-start | bytes 2359296 | tf_op jit(solution)/shard_map/all_gather | solution.py:129
  204.0 144.6 %all-gather.39.cloned.1.call-start = ((), (), s32[]{:S(2)}) async-start(), calls=%async_computation.32 | async-start | bytes 2621440 | tf_op jit(solution)/shard_map/all_gather | solution.py:32
  204.7 189.4 %reduce-scatter.41.cloned.1.call-start = ((), (), s32[]{:S(2)}) async-start(), calls=%async_computation.33 | async-start | bytes 2621440 | tf_op jit(solution)/shard_map/reduce_scatter | solution.py:38
  348.5 10.3 copy-start.51
  362.6 60.1 %all-gather.41.cloned.1.call-start = ((), (), s32[]{:S(2)}) async-start(), calls=%async_computation.34 | async-start | bytes 2621440 | tf_op jit(solution)/shard_map/all_gather | solution.py:32
  399.9 25.3 %copy-start.9 = (bf16[1,1024,4,192]{1,3,2,0:T(8,128)(2,1)S(1)}, bf16[1,1024,4,192]{1,3,2,0:T(8,128)(2,1)}, u32[]{:S(2)}) copy-start(bf16[1,1024,4,192]{1,3,2,0:T(8,128)(2,1)} %copy-done.8) | copy-start | bytes 4718596
  399.9 91.8 %reduce-scatter.43.cloned.1.call-start = ((), (), s32[]{:S(2)}) async-start(), calls=%async_computation.35 | async-start | bytes 2621440 | tf_op jit(solution)/shard_map/reduce_scatter | solution.py:38
  425.1 7.7 slice-start
  425.1 7.7 slice-start.1
  432.8 6.9 slice-start.2
  432.9 6.9 slice-start.3
  460.1 59.4 %all-gather.21.cloned.1.call-start = ((), (), s32[]{:S(2)}) async-start(), calls=%async_computation.17 | async-start | bytes 2621440 | tf_op jit(solution)/shard_map/all_gather | solution.py:32
  496.8 71.8 %reduce-scatter.29.cloned.1.call-start = ((), (), s32[]{:S(2)}) async-start(), calls=%async_computation.19 | async-start | bytes 2621440 | tf_op jit(solution)/shard_map/reduce_scatter | solution.py:38
  523.0 8.8 copy-start.10
  525.8 6.0 copy-start.3
  534.9 35.6 %copy-start.14 = (bf16[2,256,1024]{2,1,0:T(8,128)(2,1)S(1)}, bf16[2,256,1024]{2,1,0:T(8,128)(2,1)}, u32[]{:S(2)}) copy-start(bf16[2,256,1024]{2,1,0:T(8,128)(2,1)} %param.15) | copy-start | bytes 3145732
  537.0 59.4 %all-gather.25.cloned.1.call-start = ((), (), s32[]{:S(2)}) async-start(), calls=%async_computation.20 | async-start | bytes 2621440 | tf_op jit(solution)/shard_map/all_gather | solution.py:32
  573.7 47.3 %all-gather.35.cloned.1.call-start = ((), (), s32[]{:S(2)}) async-start(), calls=%async_computation.28 | async-start | bytes 2621440 | tf_op jit(solution)/shard_map/all_gather | solution.py:32
  574.3 91.8 %reduce-scatter.37.cloned.1.call-start = ((), (), s32[]{:S(2)}) async-start(), calls=%async_computation.29 | async-start | bytes 2621440 | tf_op jit(solution)/shard_map/reduce_scatter | solution.py:38
  621.0 9.7 copy-start.52
  634.5 59.4 %all-gather.37.cloned.1.call-start = ((), (), s32[]{:S(2)}) async-start(), calls=%async_computation.30 | async-start | bytes 2621440 | tf_op jit(solution)/shard_map/all_gather | solution.py:32
  671.2 118.8 %reduce-scatter.39.cloned.1.call-start = ((), (), s32[]{:S(2)}) async-start(), calls=%async_computation.31 | async-start | bytes 2621440 | tf_op jit(solution)/shard_map/reduce_scatter | solution.py:38
  696.5 7.7 slice-start.4
  696.5 7.7 slice-start.5
  704.2 6.9 slice-start.6
  704.2 6.9 slice-start.7
  731.0 72.6 %reduce-scatter.35.cloned.1.call-start = ((), (), s32[]{:S(2)}) async-start(), calls=%async_computation.27 | async-start | bytes 2621440 | tf_op jit(solution)/shard_map/reduce_scatter | solution.py:38
  738.6 7.6 copy-start.57
  738.6 8.8 copy-start.56
  738.6 9.1 copy-start.17
  738.6 10.2 copy-start.41
  738.6 10.2 copy-start.45
  738.6 92.0 %reduce-scatter.31.cloned.1.call-start = ((), (), s32[]{:S(2)}) async-start(), calls=%async_computation.23 | async-start | bytes 2621440 | tf_op jit(solution)/shard_map/reduce_scatter | solution.py:38
  746.1 159.8 %reduce-scatter.45.cloned.1.call-start = ((), (), s32[]{:S(2)}) async-start(), calls=%async_computation.36 | async-start | bytes 40960 | tf_op jit(solution)/shard_map/reduce_scatter | solution.py:323
  748.8 7.9 copy-start.42
  792.1 6.8 copy-start.18
  795.1 6.0 copy-start.7
  795.1 6.0 copy-start.37
  859.2 91.1 %reduce-scatter.59.cloned.1.call-start = ((), (), s32[]{:S(2)}) async-start(), calls=%async_computation.43 | async-start | bytes 2359296
  871.6 149.8 %reduce-scatter.47.cloned.1.call-start = ((), (), s32[]{:S(2)}) async-start(), calls=%async_computation.37 | async-start | bytes 2359296 | tf_op jit(solution)/shard_map/reduce_scatter | solution.py:359
  880.7 197.2 %reduce-scatter.55.cloned.1.call-start = ((), (), s32[]{:S(2)}) async-start(), calls=%async_computation.41 | async-start | bytes 36864
  886.9 256.2 %reduce-scatter.57.cloned.1.call-start = ((), (), s32[]{:S(2)}) async-start(), calls=%async_computation.42 | async-start | bytes 589824
  895.6 314.7 %reduce-scatter.53.cloned.1.call-start = ((), (), s32[]{:S(2)}) async-start(), calls=%async_computation.40 | async-start | bytes 1769472
  905.8 368.3 %reduce-scatter.51.cloned.1.call-start = ((), (), s32[]{:S(2)}) async-start(), calls=%async_computation.39 | async-start | bytes 73728
  907.4 444.0 %reduce-scatter.49.cloned.1.call-start = ((), (), s32[]{:S(2)}) async-start(), calls=%async_computation.38 | async-start | bytes 3538944
  917.7 6.2 copy-start.44
  917.7 6.3 copy-start.43
  (33 other events, 116.8 us)
Sparse Core Ops, SparseCore 0:
  10.2 63.3 all-gather.18
  75.6 44.9 all-gather.22
  122.7 25.8 all-gather.30
  166.0 31.4 reduce-scatter.32
  199.6 49.2 all-gather.26
  251.0 21.0 all-gather.32
  274.4 51.0 all-gather.28
  327.7 20.7 all-gather.38
  362.7 31.3 reduce-scatter.40
  400.0 22.6 all-gather.40
  460.3 31.4 reduce-scatter.42
  497.0 22.5 all-gather.20
  537.1 31.4 reduce-scatter.28
  573.8 22.5 all-gather.24
  598.4 22.5 all-gather.34
  634.6 31.4 reduce-scatter.36
  671.3 22.5 all-gather.36
  731.1 31.5 reduce-scatter.38
  765.2 31.3 reduce-scatter.34
  799.2 31.4 reduce-scatter.30
  859.3 19.3 reduce-scatter.44
  882.6 67.5 reduce-scatter.58
  954.8 66.6 reduce-scatter.46
  1025.3 52.5 reduce-scatter.54
  1082.2 60.8 reduce-scatter.56
  1146.4 63.9 reduce-scatter.52
  1213.9 60.1 reduce-scatter.50
  1278.1 73.2 reduce-scatter.48
where the time goes:
time: 1370 us; the launch traced here: 1360 us
  waiting for transfers between devices  831 us (61%)
  matrix products  187 us (14%)
  blocking collectives  166 us (12%)
  other arithmetic  99.5 us (7%)
  local copies, waits for them, and re-layouts  57.1 us (4%)
  between operations  18.7 us (1%)
    unnamed x34, waiting for transfers between devices  335 us
    all_gather x8, waiting for transfers between devices, gather_rows(): lax.all_gather(as_sent(value), 'tensor', axis=0, tiled=True)  167 us
    reduce_scatter x8, waiting for transfers between devices, sum_rows(): lax.psum_scatter(value.astype(jnp.bfloat16), 'tensor', scatter_dimension=...  156 us
    reduce_scatter x1, waiting for transfers between devices, body(): lax.psum_scatter(acc_fc_in.astype(jnp.bfloat16), 'dp', scatter_dimension=...  69.3 us
    unnamed x3, blocking collectives  49.2 us
    all_gather x1, waiting for transfers between devices, mlp_params(): lax.all_gather(shrink_weight, 'dp', axis=1, tiled=True)  46.8 us
    unnamed x166, local copies, waits for them, and re-layouts  43.6 us
    all_gather x1, waiting for transfers between devices, body(): lax.all_gather(adaptive_weight, 'dp', axis=1, tiled=True)  33.8 us
  transfers between devices with their start and end apart: 28, of which 24 were waited for; matrix products, arithmetic and copies ran while one was open for 11% of the time, Pallas kernels for 0%

commit v1 on v0

--- a/solution.py
+++ b/solution.py
@@ -6,14 +6,6 @@
 epsilon = 1e-06
 
 
-def as_sent(array):
-
-    def short(part):
-        return part.astype(jnp.bfloat16) if part.dtype == jnp.float32 else part
-
-    return jax.tree.map(short, array)
-
-
 def normalize(value):
     centered = value - jnp.mean(value, axis=-1, keepdims=True)
     inverse = lax.rsqrt(jnp.mean(centered * centered, axis=-1, keepdims=True) + epsilon)
@@ -27,17 +19,58 @@
 
 
 def gather_rows(value):
-    return jax.tree.map(
-        lambda part, own: part.astype(own.dtype),
-        lax.all_gather(as_sent(value), "tensor", axis=0, tiled=True),
-        value,
-    )
+    size = lax.axis_size("tensor")
+    me = lax.axis_index("tensor")
+    parts = value[None]
+    bit = size // 2
+    while bit >= 1:
+        other = lax.ppermute(parts, "tensor", [(one, one ^ bit) for one in range(size)])
+        low = lax.rem(me // bit, 2) == 0
+        parts = jnp.stack(
+            [jnp.where(low, parts, other), jnp.where(low, other, parts)], axis=1
+        ).reshape(2 * parts.shape[0], *value.shape)
+        bit //= 2
+    return parts.reshape(size * value.shape[0], *value.shape[1:])
 
 
 def sum_rows(value):
-    return lax.psum_scatter(
-        value.astype(jnp.bfloat16), "tensor", scatter_dimension=0, tiled=True
-    ).astype(jnp.float32)
+    size = lax.axis_size("tensor")
+    me = lax.axis_index("tensor")
+    parts = value.reshape(size, value.shape[0] // size, *value.shape[1:])
+    bit = 1
+    while bit < size:
+        pairs = parts.reshape(parts.shape[0] // 2, 2, *parts.shape[1:])
+        low = lax.rem(me // bit, 2) == 0
+        keep = jnp.where(low, pairs[:, 0], pairs[:, 1])
+        send = jnp.where(low, pairs[:, 1], pairs[:, 0]).astype(jnp.bfloat16)
+        other = lax.ppermute(send, "tensor", [(one, one ^ bit) for one in range(size)])
+        parts = keep + other.astype(jnp.float32)
+        bit *= 2
+    return parts[0]
+
+
+def shifted(size, step):
+    return [(source, (source + step) % size) for source in range(size)]
+
+
+def exchange_dp(pick):
+    size = lax.axis_size("dp")
+    me = lax.axis_index("dp")
+    return [pick(me)] + [
+        lax.ppermute(pick(lax.rem(me + step, size)), "dp", shifted(size, step))
+        for step in range(1, size)
+    ]
+
+
+def by_source(parts):
+    size = lax.axis_size("dp")
+    me = lax.axis_index("dp")
+    order = lax.rem(me + size - jnp.arange(size, dtype=jnp.int32), size)
+    return jnp.take(jnp.stack(parts), order, axis=0, mode="clip")
+
+
+def at(value, index):
+    return lax.dynamic_index_in_dim(value, index, 0, keepdims=False)
 
 
 def attend_forward(query, keys, values, block, scale):
@@ -130,17 +163,32 @@
         )
         return pieces
 
-    ada_full, ada_bias, outward_piece, shrink_piece = (
-        lax.all_gather(adaptive_weight, "dp", axis=1, tiled=True),
-        lax.all_gather(adaptive_bias, "dp", axis=1, tiled=True),
-        lax.all_gather(outward_bias, "dp", axis=0, tiled=True),
-        lax.all_gather(shrink_bias, "dp", axis=0, tiled=True),
-    )
+    dp_size = lax.axis_size("dp")
+    dp_at = lax.axis_index("dp")
+    pairs = micro * latents
+    rows_piece = adaptive_weight.shape[1]
+    cols_piece = adaptive_weight.shape[2]
     cond_float = condition.astype(jnp.float32)
     cond_act = jax.nn.silu(cond_float).astype(jnp.bfloat16)
-    mod_part = jnp.einsum(
-        "bli,kio->blko", cond_act, ada_full, preferred_element_type=jnp.float32
-    ) + ada_bias.astype(jnp.float32)
+    packet = jnp.concatenate(
+        [
+            jnp.pad(part.reshape(-1, outward_bias.shape[0]), ((0, 0), (0, 128 - outward_bias.shape[0])))
+            for part in (adaptive_bias, outward_bias, shrink_bias)
+        ]
+    )
+    spread = by_source(exchange_dp(lambda target: packet))[:, :, : outward_bias.shape[0]]
+    ada_bias = spread[:, :6].transpose(1, 0, 2).reshape(6, cols_piece)
+    outward_piece = spread[:, 6].reshape(-1)
+    shrink_piece = spread[:, 7].reshape(-1)
+    cond_all = by_source(exchange_dp(lambda target: cond_act.reshape(pairs, width)))
+    cond_mine = lax.dynamic_slice_in_dim(
+        cond_all.reshape(dp_size * pairs, width), dp_at * rows_piece, rows_piece, 1
+    )
+    partial = jnp.einsum(
+        "bi,kio->bko", cond_mine, adaptive_weight, preferred_element_type=jnp.float32
+    ).reshape(dp_size, pairs, 6, cols_piece)
+    mod_part = sum(exchange_dp(lambda target: at(partial, target)))
+    mod_part = mod_part.reshape(micro, latents, 6, cols_piece) + ada_bias.astype(jnp.float32)
     modulation, proj_bias, out_bias = (
         lax.all_gather(mod_part, "tensor", axis=3, tiled=True),
         lax.all_gather(outward_piece.astype(jnp.float32), "tensor", axis=0, tiled=True),
@@ -331,19 +379,28 @@
         ).astype(jnp.float32),
     )
     mod_low = mod_share.astype(jnp.bfloat16)
-    grad_ada = jnp.einsum("bli,blko->kio", cond_act, mod_low, preferred_element_type=jnp.float32)
-    grad_ada_bias = jnp.sum(mod_low, axis=(0, 1), dtype=jnp.float32)
-    cond_back = jnp.einsum("blko,kio->bli", mod_low, ada_full, preferred_element_type=jnp.float32)
-    cond_total = lax.psum(cond_back.astype(jnp.bfloat16), "tensor").astype(jnp.float32)
+    mod_all = by_source(
+        exchange_dp(lambda target: mod_low.reshape(pairs, 6, cols_piece))
+    ).reshape(dp_size * pairs, 6, cols_piece)
+    grad_ada = jnp.einsum("bi,bko->kio", cond_mine, mod_all, preferred_element_type=jnp.float32)
+    grad_ada_bias = lax.dynamic_slice_in_dim(
+        jnp.sum(mod_all, axis=0, dtype=jnp.float32),
+        dp_at * adaptive_bias.shape[1],
+        adaptive_bias.shape[1],
+        1,
+    )
+    cond_back = jnp.einsum(
+        "bko,kio->bi", mod_all, adaptive_weight, preferred_element_type=jnp.float32
+    ).reshape(dp_size, pairs, rows_piece)
+    cond_mix = by_source(exchange_dp(lambda target: at(cond_back, target)))
+    cond_total = lax.psum(
+        cond_mix.transpose(1, 0, 2).reshape(condition.shape).astype(jnp.bfloat16), "tensor"
+    ).astype(jnp.float32)
     unused, pull_cond = jax.vjp(jax.nn.silu, cond_float)
     grad_cond = pull_cond(cond_total)[0]
     shares = (
-        lax.psum_scatter(
-            grad_ada.astype(jnp.bfloat16), "dp", scatter_dimension=1, tiled=True
-        ).astype(jnp.float32),
-        lax.psum_scatter(
-            grad_ada_bias.astype(jnp.bfloat16), "dp", scatter_dimension=1, tiled=True
-        ).astype(jnp.float32),
+        grad_ada,
+        grad_ada_bias,
         lax.psum_scatter(
             acc_qkv.astype(jnp.bfloat16), "dp", scatter_dimension=0, tiled=True
         ).astype(jnp.float32),

time: 1370 us -> 939 us (0.69)
  waiting for transfers between devices: 831 us -> 383 us
  starting transfers between devices: 3.19 us -> 67.8 us
  blocking collectives: 166 us -> 116 us
  matrix products: 187 us -> 152 us
  local copies, waits for them, and re-layouts: 57.1 us -> 88.5 us
    unnamed x34 -> x14, waiting for transfers between devices: 335 us -> 82.3 us
    ppermute x0 -> x67, waiting for transfers between devices: none -> 234 us  [the longest x16 101 us: gather_rows(): lax.ppermute(parts, 'tensor', [(one, one ^ bit) for one in range(size)])]
    all_gather x9 -> x0, waiting for transfers between devices: 201 us -> none  [the longest x8 167 us: gather_rows(): lax.all_gather(as_sent(value), 'tensor', axis=0, tiled=True)]
    reduce_scatter x9 -> x0, waiting for transfers between devices: 156 us -> none  [the longest x8 156 us: sum_rows(): lax.psum_scatter(value.astype(jnp.bfloat16), 'tensor', scatter_dimension=...]
    ppermute x0 -> x67, starting transfers between devices: none -> 67.1 us  [the longest x35 43.7 us: exchange_dp(): lax.ppermute(pick(lax.rem(me + step, size)), 'dp', shifted(size, step))]
    all_gather x1, waiting for transfers between devices: 46.8 us -> 0.01 us  [mlp_params(): lax.all_gather(shrink_weight, 'dp', axis=1, tiled=True)]
    unnamed x3 -> x1, blocking collectives: 49.2 us -> 18.2 us
    all_gather x1 -> x0, blocking collectives: 28.2 us -> none  [body(): lax.all_gather(adaptive_bias, 'dp', axis=1, tiled=True)]
  transfers between devices with their start and end apart: 28 -> 76, of which waited for: 24 -> 42; matrix products, arithmetic and copies ran while one was open for 11% -> 21% of each run, Pallas kernels for 0% -> 0%
where the time goes in v1:
time: 939 us; the launch traced here: 933 us
  waiting for transfers between devices  383 us (41%)
  matrix products  152 us (16%)
  blocking collectives  116 us (12%)
  other arithmetic  106 us (11%)
  local copies, waits for them, and re-layouts  88.5 us (9%)
  starting transfers between devices  67.8 us (7%)
  between operations  19.4 us (2%)
    ppermute x16, waiting for transfers between devices, gather_rows(): lax.ppermute(parts, 'tensor', [(one, one ^ bit) for one in range(size)])  101 us
    unnamed x14, waiting for transfers between devices  82.3 us
    ppermute x16, waiting for transfers between devices, sum_rows(): lax.ppermute(send, 'tensor', [(one, one ^ bit) for one in range(size)])  74.4 us
    reduce_scatter x1, waiting for transfers between devices, body(): lax.psum_scatter(acc_fc_in.astype(jnp.bfloat16), 'dp', scatter_dimension=...  66.6 us
    ppermute x35, waiting for transfers between devices, exchange_dp(): lax.ppermute(pick(lax.rem(me + step, size)), 'dp', shifted(size, step))  59.2 us
    unnamed x403, local copies, waits for them, and re-layouts  55.7 us
    ppermute x35, starting transfers between devices, exchange_dp(): lax.ppermute(pick(lax.rem(me + step, size)), 'dp', shifted(size, step))  43.7 us
    all_gather x1, blocking collectives, attn_params(): lax.all_gather(outward_weight, 'dp', axis=2, tiled=True)  29.8 us
  transfers between devices with their start and end apart: 76, of which 42 were waited for; matrix products, arithmetic and copies ran while one was open for 21% of the time, Pallas kernels for 0%

profile of v1, /device:TPU:0, one launch (start us, length us, event | category | flops | bytes accessed | tf_op | source)
XLA Modules:
  0.0 933.1 jit_solution(3389806379423799498)
XLA Ops:
  8.0 6.0 collective-permute-start.6
  24.6 5.5 collective-permute-done.15
  30.1 5.4 collective-permute-done.16
  35.5 4.5 collective-permute-done.17
  40.0 4.5 collective-permute-done.18
  49.4 5.1 collective-permute-done
  54.4 5.4 collective-permute-done.1
  59.9 5.4 collective-permute-done.2
  71.1 4.2 collective-permute-start.10
  75.9 4.1 collective-permute-start.13
  81.4 5.2 all-gather
  94.9 12.7 %collective-permute-done.21 = bf16[1,256,1024]{2,1,0:T(8,128)(2,1)S(1)} collective-permute-done((bf16[1,256,1024]{2,1,0:T(8,128)(2,1)S(1)}, bf16[1,256,1024]{2,1,0:T(8,128)(2,1)S(1)}, u32[]{:S(2)}, u32[]{:S(2)}) %collective-permute-start.21) | collective-permute-done | bytes 524320 | tf_op jit(solution)/shard_map/ppermute | solution.py:27
  108.8 21.5 %all-gather.1 = bf16[8,16,4]{1,2,0:T(4,128)(2,1)S(1)} all-gather(bf16[1,16,4]{1,2,0:T(4,128)(2,1)} %bitcast.1205), channel_id=1, replica_groups=mesh['dp'=8,'tensor'=4] {'dp'}, dimensions={0}, use_global_device_ids=true | all-gather | bytes 1152 | tf_op jit(solution)/shard_map/all_gather | solution.py:154
  130.6 29.8 %all_gather.21 = bf16[4,64,1024]{2,1,0:T(8,128)(2,1)S(1)} all-gather(bf16[4,64,128]{2,1,0:T(8,128)(2,1)} %param.20), channel_id=1, replica_groups=mesh['dp'=8,'tensor'=4] {'dp'}, dimensions={2}, use_global_device_ids=true | all-gather | bytes 589824 | tf_op jit(solution)/shard_map/all_gather | solution.py:155
  163.6 3.9 fusion.62
  187.9 12.1 %all-gather.2 = f32[4,1,256]{2,1,0:T(1,128)S(1)} all-gather(f32[1,1,256]{2,1,0:T(1,128)S(1)} %reshape.1802), channel_id=1, replica_groups=mesh['dp'=8,'tensor'=4] {'tensor'}, dimensions={0}, use_global_device_ids=true | all-gather | bytes 5120 | tf_op jit(solution)/shard_map/all_gather | solution.py:194
  208.9 12.7 %collective-permute-done.25 = bf16[1,256,1024]{2,1,0:T(8,128)(2,1)S(1)} collective-permute-done((bf16[1,256,1024]{2,1,0:T(8,128)(2,1)S(1)}, bf16[1,256,1024]{2,1,0:T(8,128)(2,1)S(1)}, u32[]{:S(2)}, u32[]{:S(2)}) %collective-permute-start.25) | collective-permute-done | bytes 524320 | tf_op jit(solution)/shard_map/ppermute | solution.py:27
  221.9 10.4 %collective-permute-done.37 = bf16[1,256,1024]{2,1,0:T(8,128)(2,1)S(1)} collective-permute-done((bf16[1,256,1024]{2,1,0:T(8,128)(2,1)S(1)}, bf16[1,256,1024]{2,1,0:T(8,128)(2,1)S(1)}, u32[]{:S(2)}, u32[]{:S(2)}) %collective-permute-start.37) | collective-permute-done | bytes 524320 | tf_op jit(solution)/shard_map/ppermute | solution.py:27
  232.6 17.5 %all-gather.3 = bf16[8,1,128]{2,1,0:T(2,128)(2,1)S(1)} all-gather(bf16[1,1,128]{2,1,0:T(2,128)(2,1)S(1)} %bitcast.1222), channel_id=1, replica_groups=mesh['dp'=8,'tensor'=4] {'dp'}, dimensions={0}, use_global_device_ids=true | all-gather | bytes 2304 | tf_op jit(solution)/shard_map/all_gather | solution.py:161
  253.8 6.5 fusion.291
  260.4 9.0 convert_reduce_fusion.1
  280.3 5.4 all-gather.4
  294.2 9.8 %collective-permute-done.40 = bf16[1,256,1024]{2,1,0:T(8,128)(2,1)S(1)} collective-permute-done((bf16[1,256,1024]{2,1,0:T(8,128)(2,1)S(1)}, bf16[1,256,1024]{2,1,0:T(8,128)(2,1)S(1)}, u32[]{:S(2)}, u32[]{:S(2)}) %collective-permute-start.40) | collective-permute-done | bytes 524320 | tf_op jit(solution)/shard_map/ppermute | solution.py:46
  304.6 10.0 %collective-permute-done.28 = bf16[1,256,1024]{2,1,0:T(8,128)(2,1)S(1)} collective-permute-done((bf16[1,256,1024]{2,1,0:T(8,128)(2,1)S(1)}, bf16[1,256,1024]{2,1,0:T(8,128)(2,1)S(1)}, u32[]{:S(2)}, u32[]{:S(2)}) %collective-permute-start.28) | collective-permute-done | bytes 524320 | tf_op jit(solution)/shard_map/ppermute | solution.py:46
  317.8 12.0 %collective-permute-done.41 = bf16[1,256,1024]{2,1,0:T(8,128)(2,1)S(1)} collective-permute-done((bf16[1,256,1024]{2,1,0:T(8,128)(2,1)S(1)}, bf16[1,256,1024]{2,1,0:T(8,128)(2,1)S(1)}, u32[]{:S(2)}, u32[]{:S(2)}) %collective-permute-start.41) | collective-permute-done | bytes 524320 | tf_op jit(solution)/shard_map/ppermute | solution.py:27
  338.0 4.5 multiply_reduce_fusion.3
  342.5 4.7 multiply_convert_fusion.3
  365.6 4.3 dot_general.269
  369.9 3.7 convolution_bitcast_fusion.1
  378.9 12.7 %collective-permute-done.44 = bf16[1,256,1024]{2,1,0:T(8,128)(2,1)S(1)} collective-permute-done((bf16[1,256,1024]{2,1,0:T(8,128)(2,1)S(1)}, bf16[1,256,1024]{2,1,0:T(8,128)(2,1)S(1)}, u32[]{:S(2)}, u32[]{:S(2)}) %collective-permute-start.44) | collective-permute-done | bytes 524320 | tf_op jit(solution)/shard_map/ppermute | solution.py:46
  398.2 11.8 %collective-permute-done.29 = bf16[1,256,1024]{2,1,0:T(8,128)(2,1)S(1)} collective-permute-done((bf16[1,256,1024]{2,1,0:T(8,128)(2,1)S(1)}, bf16[1,256,1024]{2,1,0:T(8,128)(2,1)S(1)}, u32[]{:S(2)}, u32[]{:S(2)}) %collective-permute-start.29) | collective-permute-done | bytes 524320 | tf_op jit(solution)/shard_map/ppermute | solution.py:27
  436.0 12.7 %collective-permute-done.32 = bf16[1,256,1024]{2,1,0:T(8,128)(2,1)S(1)} collective-permute-done((bf16[1,256,1024]{2,1,0:T(8,128)(2,1)S(1)}, bf16[1,256,1024]{2,1,0:T(8,128)(2,1)S(1)}, u32[]{:S(2)}, u32[]{:S(2)}) %collective-permute-start.32) | collective-permute-done | bytes 524320 | tf_op jit(solution)/shard_map/ppermute | solution.py:46
  454.6 12.8 %collective-permute-done.33 = bf16[1,256,1024]{2,1,0:T(8,128)(2,1)S(1)} collective-permute-done((bf16[1,256,1024]{2,1,0:T(8,128)(2,1)S(1)}, bf16[1,256,1024]{2,1,0:T(8,128)(2,1)S(1)}, u32[]{:S(2)}, u32[]{:S(2)}) %collective-permute-start.33) | collective-permute-done | bytes 524320 | tf_op jit(solution)/shard_map/ppermute | solution.py:27
  467.7 9.2 collective-permute-done.45
  484.6 5.7 convert_reduce_fusion
  501.1 11.0 %collective-permute-done.48 = bf16[1,256,1024]{2,1,0:T(8,128)(2,1)S(1)} collective-permute-done((bf16[1,256,1024]{2,1,0:T(8,128)(2,1)S(1)}, bf16[1,256,1024]{2,1,0:T(8,128)(2,1)S(1)}, u32[]{:S(2)}, u32[]{:S(2)}) %collective-permute-start.48) | collective-permute-done | bytes 524320 | tf_op jit(solution)/shard_map/ppermute | solution.py:46
  512.7 9.8 %collective-permute-done.36 = bf16[1,256,1024]{2,1,0:T(8,128)(2,1)S(1)} collective-permute-done((bf16[1,256,1024]{2,1,0:T(8,128)(2,1)S(1)}, bf16[1,256,1024]{2,1,0:T(8,128)(2,1)S(1)}, u32[]{:S(2)}, u32[]{:S(2)}) %collective-permute-start.36) | collective-permute-done | bytes 524320 | tf_op jit(solution)/shard_map/ppermute | solution.py:46
  525.7 11.8 %collective-permute-done.49 = bf16[1,256,1024]{2,1,0:T(8,128)(2,1)S(1)} collective-permute-done((bf16[1,256,1024]{2,1,0:T(8,128)(2,1)S(1)}, bf16[1,256,1024]{2,1,0:T(8,128)(2,1)S(1)}, u32[]{:S(2)}, u32[]{:S(2)}) %collective-permute-start.49) | collective-permute-done | bytes 524320 | tf_op jit(solution)/shard_map/ppermute | solution.py:27
  537.9 5.0 fusion.275
  548.2 4.9 multiply_reduce_fusion.1
  553.0 4.7 multiply_convert_fusion.1
  575.7 8.5 add_convert_fusion
  584.2 3.9 copy.212
  588.2 4.8 fusion.296
  593.1 3.9 add_convert_fusion.1
  604.3 3.9 dot_general.283
  608.2 3.9 convolution_bitcast_fusion
  628.9 5.6 fusion.298
  648.5 6.9 copy.180
  655.4 5.8 fusion.6
  661.2 6.6 copy.181
  667.8 5.8 fusion.4
  678.4 4.5 add_convert_fusion.2
  688.3 8.9 reduce-scatter.27.cloned.1.call-done
  700.7 66.6 %reduce-scatter.17.cloned.1.call-done = bf16[128,1024]{1,0:T(8,128)(2,1)} async-done(((bf16[1024,1024]{1,0:T(8,128)(2,1)}), bf16[128,1024]{1,0:T(8,128)(2,1)}) %reduce-scatter.17.cloned.1.call-update) | async-done | bytes 262160 | tf_op jit(solution)/shard_map/reduce_scatter | solution.py:416
  769.1 63.1 %reduce-scatter.25.cloned.1.call-done = bf16[128,256]{1,0:T(8,128)(2,1)} async-done(((bf16[1024,256]{1,0:T(8,128)(2,1)}), bf16[128,256]{1,0:T(8,128)(2,1)}) %reduce-scatter.25.cloned.1.call-update) | async-done | bytes 65552
  837.1 3.9 convert_reduce_fusion.6
  844.3 10.2 %reduce-scatter.19.cloned.1.call-done = bf16[256,12]{1,0:T(8,128)(2,1)} async-done(((bf16[1024,12]{1,0:T(8,128)(2,1)}), bf16[256,12]{1,0:T(8,128)(2,1)}) %reduce-scatter.19.cloned.1.call-update) | async-done | bytes 6160
  855.9 4.3 collective-permute-start.59
  865.1 5.0 collective-permute-done.53
  870.1 5.4 collective-permute-done.54
  875.5 5.6 collective-permute-done.55
  897.6 6.0 all-reduce.9
  904.3 18.2 %all-reduce.8 = (bf16[256]{0:T(256)(128)(2,1)S(1)}, bf16[1024]{0:T(1024)(128)(2,1)S(1)}, bf16[256]{0:T(256)(128)(2,1)S(1)}) all-reduce(bf16[256]{0:T(256)(128)(2,1)S(1)} %dynamic-slice.3, bf16[1024]{0:T(1024)(128)(2,1)S(1)} %copy-done.136, bf16[256]{0:T(256)(128)(2,1)S(1)} %dynamic-slice.9), channel_id=8, replica_groups=mesh['dp'=8,'tensor'=4] {'dp'}, use_global_device_ids=true, to_apply=%region_39.40.clone | all-reduce | flops 1536 | bytes 6144
  (758 shorter events, 294.5 us)
Async XLA Ops:
  7.2 156.5 %all-gather.9.cloned.1.call-start = ((), (), s32[]{:S(2)}) async-start(), calls=%async_computation.6 | async-start | bytes 1769472 | tf_op jit(solution)/shard_map/all_gather | solution.py:153
  8.0 57.4 %collective-permute-start.6 = (bf16[2,1024]{1,0:T(2,128)(2,1)S(1)}, bf16[2,1024]{1,0:T(2,128)(2,1)S(1)}, u32[]{:S(2)}, u32[]{:S(2)}) collective-permute-start(bf16[2,1024]{1,0:T(2,128)(2,1)S(1)} %fusion.271), channel_id=1, source_target_pairs={{0,28},{4,0},{8,4},{12,8},{16,12},{20,16},{24,20},{28,24},{1,29},{... | collective-permute-start | bytes 12296 | tf_op jit(solution)/shard_map/ppermute | solution.py:60
  14.0 51.3 %collective-permute-start.5 = (bf16[2,1024]{1,0:T(2,128)(2,1)S(1)}, bf16[2,1024]{1,0:T(2,128)(2,1)S(1)}, u32[]{:S(2)}, u32[]{:S(2)}) collective-permute-start(bf16[2,1024]{1,0:T(2,128)(2,1)S(1)} %fusion.271), channel_id=1, source_target_pairs={{0,24},{4,28},{8,0},{12,4},{16,8},{20,12},{24,16},{28,20},{1,25},{... | collective-permute-start | bytes 12296 | tf_op jit(solution)/shard_map/ppermute | solution.py:60
  14.5 50.9 %collective-permute-start.4 = (bf16[2,1024]{1,0:T(2,128)(2,1)S(1)}, bf16[2,1024]{1,0:T(2,128)(2,1)S(1)}, u32[]{:S(2)}, u32[]{:S(2)}) collective-permute-start(bf16[2,1024]{1,0:T(2,128)(2,1)S(1)} %fusion.271), channel_id=1, source_target_pairs={{0,20},{4,24},{8,28},{12,0},{16,4},{20,8},{24,12},{28,16},{1,21},{... | collective-permute-start | bytes 12296 | tf_op jit(solution)/shard_map/ppermute | solution.py:60
  14.5 50.8 %collective-permute-start.3 = (bf16[2,1024]{1,0:T(2,128)(2,1)S(1)}, bf16[2,1024]{1,0:T(2,128)(2,1)S(1)}, u32[]{:S(2)}, u32[]{:S(2)}) collective-permute-start(bf16[2,1024]{1,0:T(2,128)(2,1)S(1)} %fusion.271), channel_id=1, source_target_pairs={{0,16},{4,20},{8,24},{12,28},{16,0},{20,4},{24,8},{28,12},{1,17},{... | collective-permute-start | bytes 12296 | tf_op jit(solution)/shard_map/ppermute | solution.py:60
  17.5 236.3 %all-gather.11.cloned.1.call-start = ((), (), s32[]{:S(2)}) async-start(), calls=%async_computation.7 | async-start | bytes 2359296 | tf_op jit(solution)/shard_map/all_gather | solution.py:160
  18.3 6.3 collective-permute-start.14
  24.6 5.5 collective-permute-start.15
  30.1 5.4 collective-permute-start.16
  48.1 6.3 collective-permute-start
  54.4 5.5 collective-permute-start.1
  59.9 5.4 collective-permute-start.2
  66.9 8.3 collective-permute-start.7
  69.0 6.9 collective-permute-start.12
  69.7 10.4 %collective-permute-start.11 = (f32[2,6,256]{2,0,1:T(2,128)S(1)}, f32[2,6,256]{2,0,1:T(2,128)S(1)}, u32[]{:S(2)}, u32[]{:S(2)}) collective-permute-start(f32[2,6,256]{2,0,1:T(2,128)S(1)} %get-tuple-element.261), channel_id=1, source_target_pairs={{0,20},{4,24},{8,28},{12,0},{16,4},{20,8},{24,12},{28,16},{1,21},{... | collective-permute-start | bytes 36872 | tf_op jit(solution)/shard_map/ppermute | solution.py:60
  71.1 9.0 collective-permute-start.10
  75.3 5.5 collective-permute-start.9
  75.3 5.5 collective-permute-start.8
  75.9 5.5 collective-permute-start.13
  93.3 14.2 %collective-permute-start.21 = (bf16[1,256,1024]{2,1,0:T(8,128)(2,1)S(1)}, bf16[1,256,1024]{2,1,0:T(8,128)(2,1)S(1)}, u32[]{:S(2)}, u32[]{:S(2)}) collective-permute-start(bf16[1,256,1024]{2,1,0:T(8,128)(2,1)S(1)} %fusion.159), channel_id=1, source_target_pairs={{0,2},{1,3},{2,0},{3,1},{4,6},{5,7},{6,4},{7,5},{8,10},{9,11},{10,... | collective-permute-start | bytes 1572872 | tf_op jit(solution)/shard_map/ppermute | solution.py:27
  108.7 51.7 %collective-permute-start.22 = (bf16[2,256,1024]{2,1,0:T(8,128)(2,1)}, bf16[2,256,1024]{2,1,0:T(8,128)(2,1)}, u32[]{:S(2)}, u32[]{:S(2)}) collective-permute-start(bf16[2,256,1024]{2,1,0:T(8,128)(2,1)} %maximum_bitcast_fusion), channel_id=1, source_target_pairs={{0,1},{1,0},{2,3},{3,2},{4,5},{5,4},{6,7},{7,6},{8,9},{9,8},{10,11... | collective-permute-start | bytes 3145736 | tf_op jit(solution)/shard_map/ppermute | solution.py:27
  108.7 151.6 %all-gather.13.cloned.1.call-start = ((), (), s32[]{:S(2)}) async-start(), calls=%async_computation.8 | async-start | bytes 2359296 | tf_op jit(solution)/shard_map/all_gather | solution.py:162
  185.0 14.9 %collective-permute-start.24 = (bf16[1,256,1024]{2,1,0:T(8,128)(2,1)S(1)}, bf16[1,256,1024]{2,1,0:T(8,128)(2,1)S(1)}, u32[]{:S(2)}, u32[]{:S(2)}) collective-permute-start(bf16[1,256,1024]{2,1,0:T(8,128)(2,1)S(1)} %fusion.207), channel_id=1, source_target_pairs={{0,2},{1,3},{2,0},{3,1},{4,6},{5,7},{6,4},{7,5},{8,10},{9,11},{10,... | collective-permute-start | bytes 1572872 | tf_op jit(solution)/shard_map/ppermute | solution.py:46
  186.4 499.3 %reduce-scatter.23.cloned.1.call-start = ((), (), s32[]{:S(2)}) async-start(), calls=%async_computation.12 | async-start | bytes 36864
  206.9 14.7 %collective-permute-start.25 = (bf16[1,256,1024]{2,1,0:T(8,128)(2,1)S(1)}, bf16[1,256,1024]{2,1,0:T(8,128)(2,1)S(1)}, u32[]{:S(2)}, u32[]{:S(2)}) collective-permute-start(bf16[1,256,1024]{2,1,0:T(8,128)(2,1)S(1)} %get-tuple-element.205), channel_id=1, source_target_pairs={{0,2},{1,3},{2,0},{3,1},{4,6},{5,7},{6,4},{7,5},{8,10},{9,11},{10,... | collective-permute-start | bytes 1572872 | tf_op jit(solution)/shard_map/ppermute | solution.py:27
  208.2 24.1 %collective-permute-start.37 = (bf16[1,256,1024]{2,1,0:T(8,128)(2,1)S(1)}, bf16[1,256,1024]{2,1,0:T(8,128)(2,1)S(1)}, u32[]{:S(2)}, u32[]{:S(2)}) collective-permute-start(bf16[1,256,1024]{2,1,0:T(8,128)(2,1)S(1)} %get-tuple-element.215), channel_id=1, source_target_pairs={{0,2},{1,3},{2,0},{3,1},{4,6},{5,7},{6,4},{7,5},{8,10},{9,11},{10,... | collective-permute-start | bytes 1572872 | tf_op jit(solution)/shard_map/ppermute | solution.py:27
  221.8 28.3 %collective-permute-start.26 = (bf16[2,256,1024]{2,1,0:T(8,128)(2,1)S(1)}, bf16[2,256,1024]{2,1,0:T(8,128)(2,1)S(1)}, u32[]{:S(2)}, u32[]{:S(2)}) collective-permute-start(bf16[2,256,1024]{2,1,0:T(8,128)(2,1)S(1)} %maximum_bitcast_fusion.1), channel_id=1, source_target_pairs={{0,1},{1,0},{2,3},{3,2},{4,5},{5,4},{6,7},{7,6},{8,9},{9,8},{10,11... | collective-permute-start | bytes 3145736 | tf_op jit(solution)/shard_map/ppermute | solution.py:27
  232.5 19.5 %collective-permute-start.38 = (bf16[2,256,1024]{2,1,0:T(8,128)(2,1)S(1)}, bf16[2,256,1024]{2,1,0:T(8,128)(2,1)S(1)}, u32[]{:S(2)}, u32[]{:S(2)}) collective-permute-start(bf16[2,256,1024]{2,1,0:T(8,128)(2,1)S(1)} %maximum_bitcast_fusion.4), channel_id=1, source_target_pairs={{0,1},{1,0},{2,3},{3,2},{4,5},{5,4},{6,7},{7,6},{8,9},{9,8},{10,11... | collective-permute-start | bytes 3145736 | tf_op jit(solution)/shard_map/ppermute | solution.py:27
  274.0 11.7 %collective-permute-start.39 = (bf16[2,256,1024]{2,1,0:T(8,128)(2,1)}, bf16[2,256,1024]{2,1,0:T(8,128)(2,1)}, u32[]{:S(2)}, u32[]{:S(2)}) collective-permute-start(bf16[2,256,1024]{2,1,0:T(8,128)(2,1)} %fusion.175), channel_id=1, source_target_pairs={{0,1},{1,0},{2,3},{3,2},{4,5},{5,4},{6,7},{7,6},{8,9},{9,8},{10,11... | collective-permute-start | bytes 3145736 | tf_op jit(solution)/shard_map/ppermute | solution.py:46
  279.1 11.5 %collective-permute-start.27 = (bf16[2,256,1024]{2,1,0:T(8,128)(2,1)S(1)}, bf16[2,256,1024]{2,1,0:T(8,128)(2,1)}, u32[]{:S(2)}, u32[]{:S(2)}) collective-permute-start(bf16[2,256,1024]{2,1,0:T(8,128)(2,1)S(1)} %fusion.164), channel_id=1, source_target_pairs={{0,1},{1,0},{2,3},{3,2},{4,5},{5,4},{6,7},{7,6},{8,9},{9,8},{10,11... | collective-permute-start | bytes 3145736 | tf_op jit(solution)/shard_map/ppermute | solution.py:46
  289.2 14.8 %collective-permute-start.40 = (bf16[1,256,1024]{2,1,0:T(8,128)(2,1)S(1)}, bf16[1,256,1024]{2,1,0:T(8,128)(2,1)S(1)}, u32[]{:S(2)}, u32[]{:S(2)}) collective-permute-start(bf16[1,256,1024]{2,1,0:T(8,128)(2,1)S(1)} %fusion.211), channel_id=1, source_target_pairs={{0,2},{1,3},{2,0},{3,1},{4,6},{5,7},{6,4},{7,5},{8,10},{9,11},{10,... | collective-permute-start | bytes 1572872 | tf_op jit(solution)/shard_map/ppermute | solution.py:46
  292.8 21.8 %collective-permute-start.28 = (bf16[1,256,1024]{2,1,0:T(8,128)(2,1)S(1)}, bf16[1,256,1024]{2,1,0:T(8,128)(2,1)S(1)}, u32[]{:S(2)}, u32[]{:S(2)}) collective-permute-start(bf16[1,256,1024]{2,1,0:T(8,128)(2,1)S(1)} %fusion.208), channel_id=1, source_target_pairs={{0,2},{1,3},{2,0},{3,1},{4,6},{5,7},{6,4},{7,5},{8,10},{9,11},{10,... | collective-permute-start | bytes 1572872 | tf_op jit(solution)/shard_map/ppermute | solution.py:46
  316.5 13.4 %collective-permute-start.41 = (bf16[1,256,1024]{2,1,0:T(8,128)(2,1)S(1)}, bf16[1,256,1024]{2,1,0:T(8,128)(2,1)S(1)}, u32[]{:S(2)}, u32[]{:S(2)}) collective-permute-start(bf16[1,256,1024]{2,1,0:T(8,128)(2,1)S(1)} %get-tuple-element.202), channel_id=1, source_target_pairs={{0,2},{1,3},{2,0},{3,1},{4,6},{5,7},{6,4},{7,5},{8,10},{9,11},{10,... | collective-permute-start | bytes 1572872 | tf_op jit(solution)/shard_map/ppermute | solution.py:27
  377.5 14.0 %collective-permute-start.44 = (bf16[1,256,1024]{2,1,0:T(8,128)(2,1)S(1)}, bf16[1,256,1024]{2,1,0:T(8,128)(2,1)S(1)}, u32[]{:S(2)}, u32[]{:S(2)}) collective-permute-start(bf16[1,256,1024]{2,1,0:T(8,128)(2,1)S(1)} %fusion.212), channel_id=1, source_target_pairs={{0,2},{1,3},{2,0},{3,1},{4,6},{5,7},{6,4},{7,5},{8,10},{9,11},{10,... | collective-permute-start | bytes 1572872 | tf_op jit(solution)/shard_map/ppermute | solution.py:46
  396.8 13.2 %collective-permute-start.29 = (bf16[1,256,1024]{2,1,0:T(8,128)(2,1)S(1)}, bf16[1,256,1024]{2,1,0:T(8,128)(2,1)S(1)}, u32[]{:S(2)}, u32[]{:S(2)}) collective-permute-start(bf16[1,256,1024]{2,1,0:T(8,128)(2,1)S(1)} %fusion.169), channel_id=1, source_target_pairs={{0,2},{1,3},{2,0},{3,1},{4,6},{5,7},{6,4},{7,5},{8,10},{9,11},{10,... | collective-permute-start | bytes 1572872 | tf_op jit(solution)/shard_map/ppermute | solution.py:27
  434.6 14.0 %collective-permute-start.32 = (bf16[1,256,1024]{2,1,0:T(8,128)(2,1)S(1)}, bf16[1,256,1024]{2,1,0:T(8,128)(2,1)S(1)}, u32[]{:S(2)}, u32[]{:S(2)}) collective-permute-start(bf16[1,256,1024]{2,1,0:T(8,128)(2,1)S(1)} %fusion.209), channel_id=1, source_target_pairs={{0,2},{1,3},{2,0},{3,1},{4,6},{5,7},{6,4},{7,5},{8,10},{9,11},{10,... | collective-permute-start | bytes 1572872 | tf_op jit(solution)/shard_map/ppermute | solution.py:46
  452.6 14.9 %collective-permute-start.33 = (bf16[1,256,1024]{2,1,0:T(8,128)(2,1)S(1)}, bf16[1,256,1024]{2,1,0:T(8,128)(2,1)S(1)}, u32[]{:S(2)}, u32[]{:S(2)}) collective-permute-start(bf16[1,256,1024]{2,1,0:T(8,128)(2,1)S(1)} %get-tuple-element.197), channel_id=1, source_target_pairs={{0,2},{1,3},{2,0},{3,1},{4,6},{5,7},{6,4},{7,5},{8,10},{9,11},{10,... | collective-permute-start | bytes 1572872 | tf_op jit(solution)/shard_map/ppermute | solution.py:27
  453.9 23.1 %collective-permute-start.45 = (bf16[1,256,1024]{2,1,0:T(8,128)(2,1)S(1)}, bf16[1,256,1024]{2,1,0:T(8,128)(2,1)S(1)}, u32[]{:S(2)}, u32[]{:S(2)}) collective-permute-start(bf16[1,256,1024]{2,1,0:T(8,128)(2,1)S(1)} %get-tuple-element.214), channel_id=1, source_target_pairs={{0,2},{1,3},{2,0},{3,1},{4,6},{5,7},{6,4},{7,5},{8,10},{9,11},{10,... | collective-permute-start | bytes 1572872 | tf_op jit(solution)/shard_map/ppermute | solution.py:27
  467.7 9.7 %collective-permute-start.34 = (bf16[2,256,1024]{2,1,0:T(8,128)(2,1)S(1)}, bf16[2,256,1024]{2,1,0:T(8,128)(2,1)S(1)}, u32[]{:S(2)}, u32[]{:S(2)}) collective-permute-start(bf16[2,256,1024]{2,1,0:T(8,128)(2,1)S(1)} %maximum_bitcast_fusion.3), channel_id=1, source_target_pairs={{0,1},{1,0},{2,3},{3,2},{4,5},{5,4},{6,7},{7,6},{8,9},{9,8},{10,11... | collective-permute-start | bytes 3145736 | tf_op jit(solution)/shard_map/ppermute | solution.py:27
  497.3 14.8 %collective-permute-start.48 = (bf16[1,256,1024]{2,1,0:T(8,128)(2,1)S(1)}, bf16[1,256,1024]{2,1,0:T(8,128)(2,1)S(1)}, u32[]{:S(2)}, u32[]{:S(2)}) collective-permute-start(bf16[1,256,1024]{2,1,0:T(8,128)(2,1)S(1)} %fusion.213), channel_id=1, source_target_pairs={{0,2},{1,3},{2,0},{3,1},{4,6},{5,7},{6,4},{7,5},{8,10},{9,11},{10,... | collective-permute-start | bytes 1572872 | tf_op jit(solution)/shard_map/ppermute | solution.py:46
  499.8 22.8 %collective-permute-start.36 = (bf16[1,256,1024]{2,1,0:T(8,128)(2,1)S(1)}, bf16[1,256,1024]{2,1,0:T(8,128)(2,1)S(1)}, u32[]{:S(2)}, u32[]{:S(2)}) collective-permute-start(bf16[1,256,1024]{2,1,0:T(8,128)(2,1)S(1)} %fusion.210), channel_id=1, source_target_pairs={{0,2},{1,3},{2,0},{3,1},{4,6},{5,7},{6,4},{7,5},{8,10},{9,11},{10,... | collective-permute-start | bytes 1572872 | tf_op jit(solution)/shard_map/ppermute | solution.py:46
  524.3 13.2 %collective-permute-start.49 = (bf16[1,256,1024]{2,1,0:T(8,128)(2,1)S(1)}, bf16[1,256,1024]{2,1,0:T(8,128)(2,1)S(1)}, u32[]{:S(2)}, u32[]{:S(2)}) collective-permute-start(bf16[1,256,1024]{2,1,0:T(8,128)(2,1)S(1)} %get-tuple-element.194), channel_id=1, source_target_pairs={{0,2},{1,3},{2,0},{3,1},{4,6},{5,7},{6,4},{7,5},{8,10},{9,11},{10,... | collective-permute-start | bytes 1572872 | tf_op jit(solution)/shard_map/ppermute | solution.py:27
  537.8 5.2 collective-permute-start.50
  575.4 121.7 %reduce-scatter.27.cloned.1.call-start = ((), (), s32[]{:S(2)}) async-start(), calls=%async_computation.14 | async-start | bytes 2359296
  588.1 179.2 %reduce-scatter.17.cloned.1.call-start = ((), (), s32[]{:S(2)}) async-start(), calls=%async_computation.9 | async-start | bytes 2359296 | tf_op jit(solution)/shard_map/reduce_scatter | solution.py:416
  597.0 235.2 %reduce-scatter.25.cloned.1.call-start = ((), (), s32[]{:S(2)}) async-start(), calls=%async_computation.13 | async-start | bytes 589824
  612.3 7.0 collective-permute-start.51
  620.9 14.2 %collective-permute-start.52 = (bf16[1,256,1024]{2,1,0:T(8,128)(2,1)}, bf16[1,256,1024]{2,1,0:T(8,128)(2,1)}, u32[]{:S(2)}, u32[]{:S(2)}) collective-permute-start(bf16[1,256,1024]{2,1,0:T(8,128)(2,1)} %fusion.214), channel_id=1, source_target_pairs={{0,2},{1,3},{2,0},{3,1},{4,6},{5,7},{6,4},{7,5},{8,10},{9,11},{10,... | collective-permute-start | bytes 1572872 | tf_op jit(solution)/shard_map/ppermute | solution.py:46
  628.8 225.6 %reduce-scatter.19.cloned.1.call-start = ((), (), s32[]{:S(2)}) async-start(), calls=%async_computation.10 | async-start | bytes 327680
  678.3 246.0 %reduce-scatter.21.cloned.1.call-start = ((), (), s32[]{:S(2)}) async-start(), calls=%async_computation.11 | async-start | bytes 1769472
  855.9 25.4 %collective-permute-start.59 = (bf16[2,6,256]{2,0,1:T(2,128)(2,1)S(1)}, bf16[2,6,256]{2,0,1:T(2,128)(2,1)S(1)}, u32[]{:S(2)}, u32[]{:S(2)}) collective-permute-start(bf16[2,6,256]{2,0,1:T(2,128)(2,1)S(1)} %bitcast.1189), channel_id=1, source_target_pairs={{0,28},{4,0},{8,4},{12,8},{16,12},{20,16},{24,20},{28,24},{1,29},{... | collective-permute-start | bytes 18440 | tf_op jit(solution)/shard_map/ppermute | solution.py:60
  860.2 21.1 %collective-permute-start.58 = (bf16[2,6,256]{2,0,1:T(2,128)(2,1)S(1)}, bf16[2,6,256]{2,0,1:T(2,128)(2,1)S(1)}, u32[]{:S(2)}, u32[]{:S(2)}) collective-permute-start(bf16[2,6,256]{2,0,1:T(2,128)(2,1)S(1)} %bitcast.1190), channel_id=1, source_target_pairs={{0,24},{4,28},{8,0},{12,4},{16,8},{20,12},{24,16},{28,20},{1,25},{... | collective-permute-start | bytes 18440 | tf_op jit(solution)/shard_map/ppermute | solution.py:60
  860.7 20.5 %collective-permute-start.57 = (bf16[2,6,256]{2,0,1:T(2,128)(2,1)S(1)}, bf16[2,6,256]{2,0,1:T(2,128)(2,1)S(1)}, u32[]{:S(2)}, u32[]{:S(2)}) collective-permute-start(bf16[2,6,256]{2,0,1:T(2,128)(2,1)S(1)} %bitcast.1191), channel_id=1, source_target_pairs={{0,20},{4,24},{8,28},{12,0},{16,4},{20,8},{24,12},{28,16},{1,21},{... | collective-permute-start | bytes 18440 | tf_op jit(solution)/shard_map/ppermute | solution.py:60
  860.7 20.5 %collective-permute-start.56 = (bf16[2,6,256]{2,0,1:T(2,128)(2,1)S(1)}, bf16[2,6,256]{2,0,1:T(2,128)(2,1)S(1)}, u32[]{:S(2)}, u32[]{:S(2)}) collective-permute-start(bf16[2,6,256]{2,0,1:T(2,128)(2,1)S(1)} %bitcast.1192), channel_id=1, source_target_pairs={{0,16},{4,20},{8,24},{12,28},{16,0},{20,4},{24,8},{28,12},{1,17},{... | collective-permute-start | bytes 18440 | tf_op jit(solution)/shard_map/ppermute | solution.py:60
  863.6 6.5 collective-permute-start.53
  870.1 5.4 collective-permute-start.54
  875.5 5.6 collective-permute-start.55
  882.4 7.1 collective-permute-start.65
  882.5 8.1 collective-permute-start.66
  883.4 9.8 %collective-permute-start.64 = (f32[2,128]{1,0:T(2,128)S(1)}, f32[2,128]{1,0:T(2,128)S(1)}, u32[]{:S(2)}, u32[]{:S(2)}) collective-permute-start(f32[2,128]{1,0:T(2,128)S(1)} %bitcast.1212), channel_id=1, source_target_pairs={{0,20},{4,24},{8,28},{12,0},{16,4},{20,8},{24,12},{28,16},{1,21},{... | collective-permute-start | bytes 3080 | tf_op jit(solution)/shard_map/ppermute | solution.py:60
  883.4 9.8 %collective-permute-start.63 = (f32[2,128]{1,0:T(2,128)S(1)}, f32[2,128]{1,0:T(2,128)S(1)}, u32[]{:S(2)}, u32[]{:S(2)}) collective-permute-start(f32[2,128]{1,0:T(2,128)S(1)} %bitcast.1210), channel_id=1, source_target_pairs={{0,16},{4,20},{8,24},{12,28},{16,0},{20,4},{24,8},{28,12},{1,17},{... | collective-permute-start | bytes 3080 | tf_op jit(solution)/shard_map/ppermute | solution.py:60
  886.9 6.3 collective-permute-start.62
  889.5 5.4 collective-permute-start.61
  890.6 6.3 collective-permute-start.60
  (191 other events, 3045.4 us)
Sparse Core Ops, SparseCore 0:
  17.6 44.5 all-gather.8
  108.9 56.9 all-gather.10
  186.5 50.0 all-gather.12
  575.6 51.3 reduce-scatter.22
  630.3 66.7 reduce-scatter.26
  700.5 66.7 reduce-scatter.16
  771.2 60.9 reduce-scatter.24
  835.4 19.0 reduce-scatter.18
  857.9 65.1 reduce-scatter.20
